TPU v7x, 1024 devices: a whole 8x8x8 slice. The times are simulated.
1024 devices in a mesh: dp: 32 (over y, x_lo), seq: 32 (over z, x_hi, core).
Axes of the slice: x: 8 (x_hi: 2, x_lo: 4; x = x_hi * 4 + x_lo), y: 8, z: 8, core: 2. Of those that a mesh axis runs over, the one named last changes fastest.
Arguments:
- queries: bfloat16 [32, 4096, 512], P('dp', 'seq'), may hold values from -6 to 6
- keys: bfloat16 [32, 4096, 512], P('dp', 'seq'), may hold values from -6 to 6
- values: bfloat16 [32, 4096, 512], P('dp', 'seq'), may hold values from -6 to 6
- gates: bfloat16 [32, 4096, 512], P('dp', 'seq'), may hold values from -6 to 6
- lengths: int32 [32], P('dp'), may hold values from 1024 to 4096, as said below
- rab_steps: float32 [4, 16], replicated, may hold values from -3 to 3
- out_grad: bfloat16 [32, 4096, 512], P('dp', 'seq'), may hold values from -6 to 6
Outputs:
- gated: bfloat16 [32, 4096, 512], P('dp', 'seq')
- query_grad: bfloat16 [32, 4096, 512], P('dp', 'seq')
- key_grad: bfloat16 [32, 4096, 512], P('dp', 'seq')
- value_grad: bfloat16 [32, 4096, 512], P('dp', 'seq')
- gate_grad: bfloat16 [32, 4096, 512], P('dp', 'seq')
- rab_grad: float32 [4, 16], replicated
Inputs may be any that keep to these rules, and one draw needn't show every extreme that they name: Events at and after position lengths[u] of user u are padding; some user fills all 4096 slots.
All inputs are finite; a program needn't handle non-finite values.
Results may differ from a plain program's by a relative error of at most 0.0057.
Values may be sent and summed in bfloat16 or wider, within the bound.
A program may use at most 64 MiB of HBM per device.

v0:
```python
import jax
import jax.numpy as jnp
from jax import lax
from jax.sharding import PartitionSpec as P


def split_heads(rows_in, head_count):
    return rows_in.reshape(rows_in.shape[0], head_count, rows_in.shape[1] // head_count)


def band_layout(query_pos, key_pos, band_width, bucket_count):
    offset = query_pos[:, None] - key_pos[None, :]
    lowest = query_pos[0] - key_pos[-1]
    base_band = jnp.clip(jnp.floor_divide(lowest, band_width), 0, bucket_count - 1)
    span = query_pos.shape[0] + key_pos.shape[0] - 1
    crossings = min(bucket_count, max(0, -(-(span - 1) // band_width)))
    return (offset, base_band, crossings)


def pair_terms(
    query_rows,
    key_rows,
    value_rows,
    dgrad_rows,
    query_pos,
    key_pos,
    rab_steps,
    valid_len,
    band_width,
    inv_root,
    attn_scale,
):
    head_count = rab_steps.shape[0]
    bucket_count = rab_steps.shape[1]
    raw_score = (
        jnp.einsum(
            "ihd,jhd->hij",
            split_heads(query_rows, head_count),
            split_heads(key_rows, head_count),
            preferred_element_type=jnp.float32,
        )
        * inv_root
    )
    offset, base_band, crossings = band_layout(query_pos, key_pos, band_width, bucket_count)
    live_mask = (offset >= 0) & (query_pos[:, None] < valid_len) & (key_pos[None, :] < valid_len)
    cumulative = jnp.cumsum(rab_steps, axis=1)
    base_bias = lax.dynamic_slice_in_dim(cumulative, base_band, 1, 1)
    bias_sum = jnp.broadcast_to(base_bias[:, :, None], raw_score.shape)
    for step_index in range(1, crossings + 1):
        level = base_band + step_index
        inside = (level < bucket_count).astype(jnp.float32)
        step_value = (
            lax.dynamic_slice_in_dim(rab_steps, jnp.minimum(level, bucket_count - 1), 1, 1) * inside
        )
        ramp_mask = (offset >= level * band_width).astype(jnp.float32)
        bias_sum = bias_sum + step_value[:, :, None] * ramp_mask[None]
    pre_act = raw_score + bias_sum
    sigmoid_pre = jax.nn.sigmoid(pre_act)
    weight = jnp.where(live_mask[None], pre_act * sigmoid_pre * attn_scale, 0.0)
    dweight = jnp.einsum(
        "ihd,jhd->hij",
        split_heads(dgrad_rows, head_count),
        split_heads(value_rows, head_count),
        preferred_element_type=jnp.float32,
    )
    dpre = jnp.where(
        live_mask[None],
        dweight * attn_scale * sigmoid_pre * (1.0 + pre_act * (1.0 - sigmoid_pre)),
        0.0,
    )
    return (weight, dpre, (offset, base_band, crossings))


def band_sums(dpre, layout, band_width, bucket_count):
    offset, base_band, crossings = layout
    band_index = jnp.arange(bucket_count, dtype=jnp.int32)[None, :]
    whole = jnp.sum(dpre, axis=(1, 2))
    result = jnp.where(band_index <= base_band, whole[:, None], 0.0)
    for step_index in range(1, crossings + 1):
        level = base_band + step_index
        ramp_mask = (offset >= level * band_width).astype(jnp.float32)
        suffix = jnp.sum(dpre * ramp_mask[None], axis=(1, 2))
        result = result + jnp.where(band_index == level, suffix[:, None], 0.0)
    return result


def in_blocks(step_fn, carry, pieces, start, row_count):
    total_rows = pieces[0].shape[0]
    limit = max(8, 65536 // row_count)
    sub_rows = 1
    for divisor in range(1, total_rows + 1):
        if total_rows % divisor == 0 and divisor <= limit:
            sub_rows = divisor
    if sub_rows == total_rows:
        return step_fn(carry, pieces[0], pieces[1], start)

    def inner(held, index):
        begin = (index * sub_rows).astype(jnp.int32)
        first_part = lax.dynamic_slice_in_dim(pieces[0], begin, sub_rows, 0)
        second_part = lax.dynamic_slice_in_dim(pieces[1], begin, sub_rows, 0)
        return (step_fn(held, first_part, second_part, start + begin), None)

    result, unused = lax.scan(inner, carry, jnp.arange(total_rows // sub_rows, dtype=jnp.int32))
    return result


def body(queries, keys, values, gates, lengths, rab_steps, out_grad):
    row_count = queries.shape[1]
    feat_width = queries.shape[2]
    head_count = rab_steps.shape[0]
    bucket_count = rab_steps.shape[1]
    total_len = row_count * lax.axis_size("seq")
    band_width = total_len // bucket_count
    inv_root = (feat_width // head_count) ** (-0.5)
    attn_scale = total_len ** (-0.5)
    first_row = lax.axis_index("seq") * row_count
    valid_len = lengths[0]
    own_query = queries[0]
    own_key = keys[0]
    own_value = values[0]
    own_gate = gates[0]
    own_outgrad = out_grad[0]
    dgrad = (own_outgrad.astype(jnp.float32) * own_gate.astype(jnp.float32)).astype(jnp.bfloat16)
    own_pos = first_row + jnp.arange(row_count, dtype=jnp.int32)

    def query_side(carry, key_piece, value_piece, start):
        attended, query_acc, rab_acc = carry
        key_pos = start + jnp.arange(key_piece.shape[0], dtype=jnp.int32)
        weight, dpre, layout = pair_terms(
            own_query,
            key_piece,
            value_piece,
            dgrad,
            own_pos,
            key_pos,
            rab_steps,
            valid_len,
            band_width,
            inv_root,
            attn_scale,
        )
        attended_new = jnp.einsum(
            "hij,jhd->ihd",
            weight.astype(jnp.bfloat16),
            split_heads(value_piece, head_count),
            preferred_element_type=jnp.float32,
        ).reshape(row_count, feat_width)
        query_new = (
            jnp.einsum(
                "hij,jhd->ihd",
                dpre.astype(jnp.bfloat16),
                split_heads(key_piece, head_count),
                preferred_element_type=jnp.float32,
            ).reshape(row_count, feat_width)
            * inv_root
        )
        return (
            attended + attended_new,
            query_acc + query_new,
            rab_acc + band_sums(dpre, layout, band_width, bucket_count),
        )

    def key_side(carry, query_piece, dgrad_piece, start):
        key_acc, value_acc = carry
        query_pos = start + jnp.arange(query_piece.shape[0], dtype=jnp.int32)
        weight, dpre, layout = pair_terms(
            query_piece,
            own_key,
            own_value,
            dgrad_piece,
            query_pos,
            own_pos,
            rab_steps,
            valid_len,
            band_width,
            inv_root,
            attn_scale,
        )
        value_new = jnp.einsum(
            "hij,ihd->jhd",
            weight.astype(jnp.bfloat16),
            split_heads(dgrad_piece, head_count),
            preferred_element_type=jnp.float32,
        ).reshape(row_count, feat_width)
        key_new = (
            jnp.einsum(
                "hij,ihd->jhd",
                dpre.astype(jnp.bfloat16),
                split_heads(query_piece, head_count),
                preferred_element_type=jnp.float32,
            ).reshape(row_count, feat_width)
            * inv_root
        )
        return (key_acc + key_new, value_acc + value_new)

    def query_step(carry, key_piece, value_piece, start):
        nothing_live = (
            (start >= first_row + row_count) | (start >= valid_len) | (first_row >= valid_len)
        )
        return lax.cond(
            nothing_live,
            lambda held: held,
            lambda held: query_side(held, key_piece, value_piece, start),
            carry,
        )

    def key_step(carry, query_piece, dgrad_piece, start):
        nothing_live = (
            (start + query_piece.shape[0] <= first_row)
            | (start >= valid_len)
            | (first_row >= valid_len)
        )
        return lax.cond(
            nothing_live,
            lambda held: held,
            lambda held: key_side(held, query_piece, dgrad_piece, start),
            carry,
        )

    zero_rows = jnp.zeros((row_count, feat_width), jnp.float32)
    zero_bias = jnp.zeros((head_count, bucket_count), jnp.float32)
    attended, query_acc, rab_acc = in_blocks(
        query_step,
        (zero_rows, zero_rows, zero_bias),
        (
            lax.all_gather(own_key, "seq", axis=0, tiled=True),
            lax.all_gather(own_value, "seq", axis=0, tiled=True),
        ),
        jnp.int32(0),
        row_count,
    )
    key_acc, value_acc = in_blocks(
        key_step,
        (zero_rows, zero_rows),
        (
            lax.all_gather(own_query, "seq", axis=0, tiled=True),
            lax.all_gather(dgrad, "seq", axis=0, tiled=True),
        ),
        jnp.int32(0),
        row_count,
    )
    rab_grad = lax.psum(rab_acc, ("dp", "seq")) / total_len
    gated = (attended * own_gate.astype(jnp.float32)).astype(jnp.bfloat16)
    gate_grad = (own_outgrad.astype(jnp.float32) * attended).astype(jnp.bfloat16)
    return (
        gated[None],
        query_acc.astype(jnp.bfloat16)[None],
        key_acc.astype(jnp.bfloat16)[None],
        value_acc.astype(jnp.bfloat16)[None],
        gate_grad[None],
        rab_grad,
    )


def solution(mesh):
    placed = (
        P("dp", "seq", None),
        P("dp", "seq", None),
        P("dp", "seq", None),
        P("dp", "seq", None),
        P("dp"),
        P(),
        P("dp", "seq", None),
    )
    return jax.shard_map(
        body,
        mesh=mesh,
        in_specs=placed,
        out_specs=(
            P("dp", "seq", None),
            P("dp", "seq", None),
            P("dp", "seq", None),
            P("dp", "seq", None),
            P("dp", "seq", None),
            P(),
        ),
        check_vma=False,
    )
```

profile of v0, /device:TPU:7, one launch (start us, length us, event | category | flops | bytes accessed | tf_op | source)
XLA Modules:
  0.0 595.4 jit_solution(10867535526679783410)
XLA Ops:
  7.2 1.7 copy.87
  9.0 1.7 copy.88
  10.7 1.7 fusion.65
  12.4 1.7 copy.92
  15.5 118.1 %all-gather.10.cloned.1.call-done = bf16[1,4096,512]{1,2,0:T(8,128)(2,1)} async-done(((bf16[1,128,512]{1,2,0:T(8,128)(2,1)}), bf16[1,4096,512]{1,2,0:T(8,128)(2,1)}) %all-gather.10.cloned.1.call-update) | async-done | bytes 4194320 | tf_op jit(solution)/shard_map/all_gather | solution.py:226
  133.6 113.7 %all-gather.12.cloned.1.call-done = bf16[1,4096,512]{1,2,0:T(8,128)(2,1)} async-done(((bf16[1,128,512]{1,2,0:T(8,128)(2,1)}), bf16[1,4096,512]{1,2,0:T(8,128)(2,1)}) %all-gather.12.cloned.1.call-update) | async-done | bytes 4194320 | tf_op jit(solution)/shard_map/all_gather | solution.py:227
  247.4 25.2 %while.32 = (s32[]{:T(128)}, f32[128,512]{0,1:T(8,128)S(1)}, f32[128,512]{0,1:T(8,128)S(1)}, f32[4,16]{1,0:T(4,128)S(1)}, s32[8]{0:T(128)S(1)}, /*index=5*/s32[]...) while((s32[]{:T(128)}, f32[128,512]{0,1:T(8,128)S(1)}, ...), condition=%wide.region_8.9_spmd.clone, body=%wide.region_0.8_spmd.clone.sunk | while | flops 277941568 | bytes 14100598 | solution.py:103
  249.3 9.6 %conditional.7 = ((f32[128,512]{0,1:T(8,128)S(1)}, f32[128,512]{0,1:T(8,128)S(1)}, f32[4,16]{1,0:T(4,128)S(1)})) conditional(s32[]{:T(128)} %convert_element_type.208, (s32[]{:T(128)}, s32[]{:T(128)}, s32[]{:T(128)}, bf16[4096,512]{0,1:T(8,128)(2,1)}, bf16[1,128,512]{2,1,0:T(8,128)(2,1)}, /*index=5*/f32[4,16]{0,1:T(8,128)S(1)}, ...), branch_computations={%region_1.6_spmd, %region_7.7_spmd} | conditional | flops 277941568 | bytes 14099764 | solution.py:200
  273.5 87.3 %all-gather.8.cloned.1.call-done = bf16[4096,512]{1,0:T(8,128)(2,1)} async-done(((bf16[128,512]{1,0:T(8,128)(2,1)}), bf16[4096,512]{1,0:T(8,128)(2,1)}) %all-gather.8.cloned.1.call-update) | async-done | bytes 4194320 | tf_op jit(solution)/shard_map/all_gather | solution.py:237
  360.8 6.5 %copy.93 = bf16[4096,512]{0,1:T(8,128)(2,1)} copy(bf16[4096,512]{1,0:T(8,128)(2,1)} %all-gather.8.cloned.1.call-done) | data formatting | bytes 8388608
  367.3 130.0 %psum.7 = f32[4,16]{1,0:T(4,128)S(1)} all-reduce(f32[4,16]{1,0:T(4,128)S(1)} %get-tuple-element.543), channel_id=1, replica_groups=mesh['dp'=32,'seq'=32] {'dp','seq'}, use_global_device_ids=true, to_apply=%region_14.15 | all-reduce | flops 64 | bytes 512 | tf_op jit(solution)/shard_map/psum | solution.py:242
  498.7 88.6 %while.33 = (s32[]{:T(128)}, f32[128,512]{0,1:T(8,128)S(1)}, f32[128,512]{0,1:T(8,128)S(1)}, s32[8]{0:T(128)S(1)}, s32[]{:T(128)}, /*index=5*/s32[]{:T(128)}, pr...) while((s32[]{:T(128)}, f32[128,512]{0,1:T(8,128)S(1)}, ...), condition=%wide.region_13.14_spmd.clone.clone, body=%wide.region_9.13_spmd.clone.clone.sunk | while | flops 276105984 | bytes 12002622 | solution.py:103
  500.7 9.1 %conditional.8 = ((f32[128,512]{0,1:T(8,128)S(1)}, f32[128,512]{0,1:T(8,128)S(1)})) conditional(s32[]{:T(128)} %convert_element_type.209, (s32[]{:T(128)}, s32[]{:T(128)}, s32[]{:T(128)}, bf16[4096,512]{0,1:T(8,128)(2,1)}, bf16[1,128,512]{2,1,0:T(8,128)(2,1)S(1)}, /*index=5*/bf16[4096,512]{0,1:T(8,128)(2,1)}, bf16[1,128,512]{2,1,0:T(8,128)(2,1)S(1)}, ...), branch_computations={%region_10.11_spmd, %region_12.12_spmd} | conditional | flops 276105984 | bytes 12001800 | solution.py:213
  507.0 1.4 constant_dynamic-slice_fusion.9
  511.7 9.1 %conditional.8 = ((f32[128,512]{0,1:T(8,128)S(1)}, f32[128,512]{0,1:T(8,128)S(1)})) conditional(s32[]{:T(128)} %convert_element_type.209, (s32[]{:T(128)}, s32[]{:T(128)}, s32[]{:T(128)}, bf16[4096,512]{0,1:T(8,128)(2,1)}, bf16[1,128,512]{2,1,0:T(8,128)(2,1)S(1)}, /*index=5*/bf16[4096,512]{0,1:T(8,128)(2,1)}, bf16[1,128,512]{2,1,0:T(8,128)(2,1)S(1)}, ...), branch_computations={%region_10.11_spmd, %region_12.12_spmd} | conditional | flops 276105984 | bytes 12001800 | solution.py:213
  518.1 1.4 constant_dynamic-slice_fusion.9
  522.8 9.1 %conditional.8 = ((f32[128,512]{0,1:T(8,128)S(1)}, f32[128,512]{0,1:T(8,128)S(1)})) conditional(s32[]{:T(128)} %convert_element_type.209, (s32[]{:T(128)}, s32[]{:T(128)}, s32[]{:T(128)}, bf16[4096,512]{0,1:T(8,128)(2,1)}, bf16[1,128,512]{2,1,0:T(8,128)(2,1)S(1)}, /*index=5*/bf16[4096,512]{0,1:T(8,128)(2,1)}, bf16[1,128,512]{2,1,0:T(8,128)(2,1)S(1)}, ...), branch_computations={%region_10.11_spmd, %region_12.12_spmd} | conditional | flops 276105984 | bytes 12001800 | solution.py:213
  533.9 9.1 %conditional.8 = ((f32[128,512]{0,1:T(8,128)S(1)}, f32[128,512]{0,1:T(8,128)S(1)})) conditional(s32[]{:T(128)} %convert_element_type.209, (s32[]{:T(128)}, s32[]{:T(128)}, s32[]{:T(128)}, bf16[4096,512]{0,1:T(8,128)(2,1)}, bf16[1,128,512]{2,1,0:T(8,128)(2,1)S(1)}, /*index=5*/bf16[4096,512]{0,1:T(8,128)(2,1)}, bf16[1,128,512]{2,1,0:T(8,128)(2,1)S(1)}, ...), branch_computations={%region_10.11_spmd, %region_12.12_spmd} | conditional | flops 276105984 | bytes 12001800 | solution.py:213
  540.3 1.4 constant_dynamic-slice_fusion.9
  545.0 9.1 %conditional.8 = ((f32[128,512]{0,1:T(8,128)S(1)}, f32[128,512]{0,1:T(8,128)S(1)})) conditional(s32[]{:T(128)} %convert_element_type.209, (s32[]{:T(128)}, s32[]{:T(128)}, s32[]{:T(128)}, bf16[4096,512]{0,1:T(8,128)(2,1)}, bf16[1,128,512]{2,1,0:T(8,128)(2,1)S(1)}, /*index=5*/bf16[4096,512]{0,1:T(8,128)(2,1)}, bf16[1,128,512]{2,1,0:T(8,128)(2,1)S(1)}, ...), branch_computations={%region_10.11_spmd, %region_12.12_spmd} | conditional | flops 276105984 | bytes 12001800 | solution.py:213
  551.3 1.4 constant_dynamic-slice_fusion.9
  556.1 9.1 %conditional.8 = ((f32[128,512]{0,1:T(8,128)S(1)}, f32[128,512]{0,1:T(8,128)S(1)})) conditional(s32[]{:T(128)} %convert_element_type.209, (s32[]{:T(128)}, s32[]{:T(128)}, s32[]{:T(128)}, bf16[4096,512]{0,1:T(8,128)(2,1)}, bf16[1,128,512]{2,1,0:T(8,128)(2,1)S(1)}, /*index=5*/bf16[4096,512]{0,1:T(8,128)(2,1)}, bf16[1,128,512]{2,1,0:T(8,128)(2,1)S(1)}, ...), branch_computations={%region_10.11_spmd, %region_12.12_spmd} | conditional | flops 276105984 | bytes 12001800 | solution.py:213
  567.2 9.1 %conditional.8 = ((f32[128,512]{0,1:T(8,128)S(1)}, f32[128,512]{0,1:T(8,128)S(1)})) conditional(s32[]{:T(128)} %convert_element_type.209, (s32[]{:T(128)}, s32[]{:T(128)}, s32[]{:T(128)}, bf16[4096,512]{0,1:T(8,128)(2,1)}, bf16[1,128,512]{2,1,0:T(8,128)(2,1)S(1)}, /*index=5*/bf16[4096,512]{0,1:T(8,128)(2,1)}, bf16[1,128,512]{2,1,0:T(8,128)(2,1)S(1)}, ...), branch_computations={%region_10.11_spmd, %region_12.12_spmd} | conditional | flops 276105984 | bytes 12001800 | solution.py:213
  578.2 9.1 %conditional.8 = ((f32[128,512]{0,1:T(8,128)S(1)}, f32[128,512]{0,1:T(8,128)S(1)})) conditional(s32[]{:T(128)} %convert_element_type.209, (s32[]{:T(128)}, s32[]{:T(128)}, s32[]{:T(128)}, bf16[4096,512]{0,1:T(8,128)(2,1)}, bf16[1,128,512]{2,1,0:T(8,128)(2,1)S(1)}, /*index=5*/bf16[4096,512]{0,1:T(8,128)(2,1)}, bf16[1,128,512]{2,1,0:T(8,128)(2,1)S(1)}, ...), branch_computations={%region_10.11_spmd, %region_12.12_spmd} | conditional | flops 276105984 | bytes 12001800 | solution.py:213
  (232 shorter events, 80.0 us)
Async XLA Ops:
  7.2 126.5 %all-gather.10.cloned.1.call-start = ((), (), s32[]{:S(2)}) async-start(), calls=%async_computation.1 | async-start | bytes 4325376 | tf_op jit(solution)/shard_map/all_gather | solution.py:226
  8.9 238.4 %all-gather.12.cloned.1.call-start = ((), (), s32[]{:S(2)}) async-start(), calls=%async_computation.2 | async-start | bytes 4325376 | tf_op jit(solution)/shard_map/all_gather | solution.py:227
  10.6 350.1 %all-gather.8.cloned.1.call-start = ((), (), s32[]{:S(2)}) async-start(), calls=%async_computation | async-start | bytes 4325376 | tf_op jit(solution)/shard_map/all_gather | solution.py:237
  12.4 486.3 %all-gather.14.cloned.1.call-start = ((), (), s32[]{:S(2)}) async-start(), calls=%async_computation.3 | async-start | bytes 4325376 | tf_op jit(solution)/shard_map/all_gather | solution.py:236
  249.3 7.6 %copy-start.2 = (bf16[128,512]{1,0:T(8,128)(2,1)S(1)}, bf16[128,512]{1,0:T(8,128)(2,1)}, u32[]{:S(2)}) copy-start(bf16[128,512]{1,0:T(8,128)(2,1)} %get-tuple-element.482) | copy-start | bytes 393220 | tf_op jit(solution)/shard_map/while/body/eval_jaxpr/cond
  273.5 224.4 %copy-start.3 = (bf16[1,128,512]{2,1,0:T(8,128)(2,1)S(1)}, bf16[1,128,512]{2,1,0:T(8,128)(2,1)}, u32[]{:S(2)}) copy-start(bf16[1,128,512]{2,1,0:T(8,128)(2,1)} %param.18) | copy-start | bytes 393220
  273.5 224.4 %copy-start.4 = (bf16[1,128,512]{2,1,0:T(8,128)(2,1)S(1)}, bf16[1,128,512]{2,1,0:T(8,128)(2,1)}, u32[]{:S(2)}) copy-start(bf16[1,128,512]{2,1,0:T(8,128)(2,1)} %param.21) | copy-start | bytes 393220
  273.5 225.2 %copy-start = (bf16[1,128,512]{2,1,0:T(8,128)(2,1)S(1)}, bf16[1,128,512]{2,1,0:T(8,128)(2,1)}, u32[]{:S(2)}) copy-start(bf16[1,128,512]{2,1,0:T(8,128)(2,1)} %param.16) | copy-start | bytes 393220
  273.5 225.2 %copy-start.1 = (bf16[1,128,512]{2,1,0:T(8,128)(2,1)S(1)}, bf16[1,128,512]{2,1,0:T(8,128)(2,1)}, u32[]{:S(2)}) copy-start(bf16[1,128,512]{2,1,0:T(8,128)(2,1)} %param.17) | copy-start | bytes 393220
Sparse Core Ops, SparseCore 0:
  12.9 120.6 all-gather.9
  138.5 108.8 all-gather.11
  252.5 108.2 all-gather.7
  364.9 108.7 all-gather.13
where the time goes:
time: 597 us; the launch traced here: 595 us
  waiting for transfers between devices  319 us (53%)
  blocking collectives  130 us (22%)
  local copies, waits for them, and re-layouts  62.4 us (10%)
  loops' own time  33.2 us (6%)
  other arithmetic  19.3 us (3%)
  matrix products  16.6 us (3%)
  between operations  14.5 us (2%)
    psum x1, blocking collectives, body(): rab_grad = lax.psum(rab_acc, ('dp', 'seq')) / total_len  130 us
    all_gather x1, waiting for transfers between devices, body(): lax.all_gather(own_key, 'seq', axis=0, tiled=True)  118 us
    all_gather x1, waiting for transfers between devices, body(): lax.all_gather(own_value, 'seq', axis=0, tiled=True)  114 us
    all_gather x1, waiting for transfers between devices, body(): lax.all_gather(dgrad, 'seq', axis=0, tiled=True)  87.3 us
    another operation x2, loops' own time, in_blocks(): lax.scan(inner, carry, jnp.arange(total_rows // sub_rows, dtype=jnp.int32))  21.6 us
    dynamic_slice x9, local copies, waits for them, and re-layouts, inner(): second_part = lax.dynamic_slice_in_dim(pieces[1], begin, sub_rows, 0)  12.3 us
    unnamed x13, local copies, waits for them, and re-layouts  12.3 us
    dynamic_slice x9, local copies, waits for them, and re-layouts, inner(): first_part = lax.dynamic_slice_in_dim(pieces[0], begin, sub_rows, 0)  12.2 us
  transfers between devices with their start and end apart: 4, of which 3 were waited for; matrix products, arithmetic and copies ran while one was open for 5% of the time, Pallas kernels for 0%

commit v1 on v0

v1 whole, which is shorter than its diff:
```python
import functools

import jax
import jax.numpy as jnp
from jax import lax
from jax.experimental import pallas as pl
from jax.experimental.pallas import tpu as pltpu
from jax.sharding import PartitionSpec as P

MESH = pl.DeviceIdType.MESH
BF16, F32 = jnp.bfloat16, jnp.float32
HEADS, DIM, BANDS = 4, 128, 16
ROWS, HALF = 128, 256
DEAD = -20000.0


def nt(a, b):
    return lax.dot_general(a, b, (((1,), (1,)), ((), ())), preferred_element_type=F32)


def nn(a, b):
    return jnp.dot(a, b, preferred_element_type=F32)


def tn(a, b):
    return lax.dot_general(a, b, (((0,), (0,)), ((), ())), preferred_element_type=F32)


def kernel(
    q_hbm, k_hbm, v_hbm, gate_hbm, og_hbm, len_ref, rab_ref,
    out_ref, rab_out,
    src, raw, obj, acc, snd, ret, stg, land, csm, low, tot,
    l_sem, a_s, a_r, f_s, f_r, b_s, b_r, o_s, o_r,
):
    sq = lax.axis_index("seq")
    z, xh, c = sq // 4, (sq // 2) % 2, sq % 2
    head = 2 * xh + c
    sign = 1 - 2 * c
    zp = c * 7 + sign * z
    prim, sec = 1 - c, c
    near, far = xh, 1 - xh

    def plane(rel):
        other_x = 1 - xh if rel & 2 else xh
        other_c = 1 - c if rel & 1 else c
        return other_x, other_c

    def at_plane(rel):
        other_x, other_c = plane(rel)
        return {"seq": z * 4 + other_x * 2 + other_c}

    def at_z(step):
        return {"seq": ((z + step * sign + 8) % 8) * 4 + xh * 2 + c}

    barrier = pltpu.get_barrier_semaphore()
    for rel in (1, 2, 3):
        pl.semaphore_signal(barrier, inc=1, device_id=at_plane(rel), device_id_type=MESH)
    for step in (1, -1, 2, -2, 3, -3):
        pl.semaphore_signal(barrier, inc=1, device_id=at_z(step), device_id_type=MESH)

    loads = [
        pltpu.make_async_copy(gate_hbm, raw.at[0], l_sem.at[0]),
        pltpu.make_async_copy(og_hbm, raw.at[1], l_sem.at[1]),
        pltpu.make_async_copy(q_hbm, src.at[0, 0], l_sem.at[2]),
        pltpu.make_async_copy(k_hbm, src.at[1, 0], l_sem.at[3]),
        pltpu.make_async_copy(v_hbm, src.at[1, 1], l_sem.at[4]),
    ]
    for load in loads:
        load.start()
    csm[0] = jnp.float32(DEAD)
    level = jnp.float32(0.0)
    for band in range(BANDS):
        level = level + rab_ref[head, band]
        csm[band + 1] = level * 0.5
    for load in loads[:2]:
        load.wait()
    row_at = sq * ROWS + lax.broadcasted_iota(jnp.int32, (ROWS, HEADS * DIM), 0)
    dgrad = raw[0].astype(F32) * raw[1].astype(F32)
    src[0, 1] = jnp.where(row_at < len_ref[0], dgrad, 0.0).astype(BF16)
    for load in loads[2:]:
        load.wait()
    pl.semaphore_wait(barrier, 9)

    def head_cols(which):
        return pl.ds(pl.multiple_of(which * DIM, DIM), DIM)

    def own_rows(which):
        return pl.ds(pl.multiple_of(which * ROWS, ROWS), ROWS)

    def exchange(rel, which):
        other_x, other_c = plane(rel)
        return pltpu.make_async_remote_copy(
            src_ref=src.at[which, :, :, head_cols(2 * other_x + other_c)],
            dst_ref=obj.at[which, xh, :, own_rows(c), :],
            send_sem=a_s.at[rel - 1, which],
            recv_sem=a_r.at[rel - 1, which],
            device_id=at_plane(rel),
            device_id_type=MESH,
        )

    def arrival(rel, which):
        other_x, other_c = plane(rel)
        return pltpu.make_async_remote_copy(
            src_ref=src.at[which, :, :, head_cols(head)],
            dst_ref=obj.at[which, other_x, :, own_rows(other_c), :],
            send_sem=a_s.at[rel - 1, which],
            recv_sem=a_r.at[rel - 1, which],
            device_id=at_plane(rel),
            device_id_type=MESH,
        )

    def leading(core):
        up = jnp.where(z >= 6, 0, 1)
        down = jnp.where(z < 2, 1, 0)
        return jnp.where(core == 0, up, down)

    mine, theirs = leading(c), leading(1 - c)
    exchange(2, mine).start()
    exchange(3, theirs).start()
    exchange(1, theirs).start()
    exchange(2, 1 - mine).start()
    exchange(3, 1 - theirs).start()
    exchange(1, 1 - theirs).start()
    for which in (0, 1):
        for part in (0, 1):
            obj[which, xh, part, own_rows(c), :] = src[which, part, :, head_cols(head)]

    def move(source, hop, dist, half, kind):
        return pltpu.make_async_remote_copy(
            src_ref=obj.at[source, half],
            dst_ref=obj.at[1 + dist, half],
            send_sem=f_s.at[kind, half],
            recv_sem=f_r.at[dist - 1, half],
            device_id=at_z(hop),
            device_id_type=MESH,
        )

    def own_slot(dist):
        return jnp.where(zp + dist < 8, prim, sec)

    def to_one(half):
        return move(own_slot(1), 1, 1, half, 0)

    def to_two(half):
        return move(own_slot(2), 2, 2, half, 1)

    def pass_three(half):
        return move(3, 1, 3, half, 2)

    def pass_four(half):
        return move(3, 2, 4, half, 3)

    def to_three(half):
        return move(sec, 3, 3, half, 4)

    gives_three = zp != 7
    gives_four = (zp >= 2) & (zp <= 5)
    has_four = zp >= 4

    def pass_on(half):
        to_two(half).wait_recv()

        @pl.when(gives_three)
        def _():
            pass_three(half).start()

        @pl.when(gives_four)
        def _():
            pass_four(half).start()

    arrival(1, mine).wait_recv()
    to_two(near).start()

    @pl.when(zp != 6)
    def _():
        to_one(near).start()

    arrival(2, mine).wait_recv()
    arrival(3, mine).wait_recv()
    to_two(far).start()

    @pl.when(zp != 6)
    def _():
        to_one(far).start()

    acc[...] = jnp.zeros_like(acc)
    low[...] = jnp.zeros_like(low)
    tot[...] = jnp.zeros_like(tot)
    pass_on(near)
    for rel in (1, 2, 3):
        arrival(rel, 1 - mine).wait_recv()

    @pl.when(zp == 6)
    def _():
        to_one(near).start()
        to_one(far).start()

    @pl.when(zp == 5)
    def _():
        to_three(near).start()
        to_three(far).start()

    pass_on(far)

    row = lax.broadcasted_iota(jnp.int32, (HALF, HALF), 0)
    col = lax.broadcasted_iota(jnp.int32, (HALF, HALF), 1)
    lower = row >= col

    def fold(tile):
        return jnp.sum(tile.reshape(HALF // 8, 8, HALF), axis=0)

    def pair(q_slot, q_half, k_slot, k_half, gap):
        query, dgr = obj[q_slot, q_half, 0], obj[q_slot, q_half, 1]
        key, value = obj[k_slot, k_half, 0], obj[k_slot, k_half, 1]
        half_act = nt(query, key) * (0.5 * DIM**-0.5) + jnp.where(lower, csm[gap + 1], csm[gap])
        th = jnp.tanh(half_act)
        up = 1.0 + th
        weight = (half_act * up).astype(BF16)
        dpre = nt(dgr, value) * (up * (1.0 + half_act * (1.0 - th)))
        dhalf = dpre.astype(BF16)
        acc[q_slot, q_half, 1] += nn(weight, value)
        acc[q_slot, q_half, 0] += nn(dhalf, key)
        acc[k_slot, k_half, 1] += tn(weight, dgr)
        acc[k_slot, k_half, 0] += tn(dhalf, query)
        tot[gap] += fold(dpre)
        low[gap] += fold(jnp.where(lower, dpre, 0.0))

    def diagonal(index, unused):
        q_half, k_half = jnp.minimum(index, 1), index // 2
        pair(0, q_half, 1, k_half, q_half - k_half)
        return unused

    lax.fori_loop(0, 3, diagonal, 0)

    def chunk(index, unused):
        dist = index // 2 + 1
        half = jnp.where(index % 2 == 0, near, far)

        @pl.when(dist != 2)
        def _():
            move(0, 1, dist, half, 0).wait_recv()

        slot = 1 + dist
        direct = zp >= dist
        kind = jnp.where(direct, prim, sec)
        gap = 2 * jnp.where(direct, dist, 8 - dist)
        q_slot = jnp.where(kind == 0, slot, 0)
        k_slot = jnp.where(kind == 0, 1, slot)
        for other in (0, 1):
            q_half = jnp.where(kind == 0, half, other)
            k_half = jnp.where(kind == 0, other, half)
            pair(q_slot, q_half, k_slot, k_half, gap + q_half - k_half)
        return unused

    lax.fori_loop(0, jnp.where(has_four, 8, 6), chunk, 0)

    def give_back(dist, hop, place, half):
        return pltpu.make_async_remote_copy(
            src_ref=snd.at[dist - 1, half],
            dst_ref=ret.at[place, half],
            send_sem=b_s.at[dist - 1, half],
            recv_sem=b_r.at[place, half],
            device_id=at_z(-hop),
            device_id_type=MESH,
        )

    def back_one(half):
        return give_back(1, 1, 2, half)

    def back_two(half):
        return give_back(2, 2, 3, half)

    def back_three(half):
        first = zp == 0
        return give_back(3, jnp.where(first, 3, 1), jnp.where(first, 4, 0), half)

    def back_four(half):
        return give_back(4, 2, 1, half)

    def ready(dist, half):
        snd[dist - 1, half] = acc[1 + dist, half].astype(BF16)

    def returned(place, half):
        give_back(1, 1, place, half).wait_recv()

    for half in (far, near):
        @pl.when(has_four)
        def _():
            ready(4, half)
            back_four(half).start()

        ready(3, half)
        back_three(half).start()
    for half in (far, near):
        ready(1, half)
        back_one(half).start()

    def deliver(rel, which):
        other_x, other_c = plane(rel)
        return pltpu.make_async_remote_copy(
            src_ref=stg.at[which, other_x, :, own_rows(other_c), :],
            dst_ref=land.at[which, :, :, head_cols(head)],
            send_sem=o_s.at[rel - 1, which],
            recv_sem=o_r.at[rel - 1, which],
            device_id=at_plane(rel),
            device_id_type=MESH,
        )

    def delivered(rel, which):
        other_x, other_c = plane(rel)
        return pltpu.make_async_remote_copy(
            src_ref=stg.at[which, other_x, :, own_rows(other_c), :],
            dst_ref=land.at[which, :, :, head_cols(2 * other_x + other_c)],
            send_sem=o_s.at[rel - 1, which],
            recv_sem=o_r.at[rel - 1, which],
            device_id=at_plane(rel),
            device_id_type=MESH,
        )

    def finish(which, half, is_far):
        stg[which, half, 0] = (acc[which, half, 0] * (DIM**-0.5 * 0.5 / 64.0)).astype(BF16)
        stg[which, half, 1] = (acc[which, half, 1] * (1.0 / 64.0)).astype(BF16)
        if is_far:
            deliver(2, which).start()
            deliver(3, which).start()
        else:
            deliver(1, which).start()
            for part in (0, 1):
                land[which, part, :, head_cols(head)] = stg[which, half, part, own_rows(c), :]

    late = own_slot(2)
    both_late = (zp == 5) | (zp == 6)

    @pl.when(jnp.logical_not(both_late))
    def _():
        finish(1 - late, far, True)
        finish(1 - late, near, False)

    for half in (far, near):
        @pl.when(gives_three)
        def _():
            returned(0, half)
            acc[3, half] += ret[0, half].astype(F32)

        @pl.when(gives_four)
        def _():
            returned(1, half)
            acc[3, half] += ret[1, half].astype(F32)

        ready(2, half)
        back_two(half).start()
    for half, is_far in ((far, True), (near, False)):
        returned(2, half)
        acc[own_slot(1), half] += ret[2, half].astype(F32)
        returned(3, half)
        acc[late, half] += ret[3, half].astype(F32)

        @pl.when(zp == 5)
        def _():
            returned(4, half)
            acc[sec, half] += ret[4, half].astype(F32)

        finish(late, half, is_far)

        @pl.when(both_late)
        def _():
            finish(1 - late, half, is_far)

    rows_out = [None] * BANDS
    running = jnp.zeros((1, HALF), F32)
    for band in range(BANDS - 1, -1, -1):
        rows_out[band] = running + jnp.sum(low[band], axis=0, keepdims=True)
        running = running + jnp.sum(tot[band], axis=0, keepdims=True)
    per_band = jnp.sum(jnp.concatenate(rows_out, axis=0), axis=1, keepdims=True)
    lane = lax.broadcasted_iota(jnp.int32, (BANDS, DIM), 1)
    line = lax.broadcasted_iota(jnp.int32, (BANDS, DIM), 0)
    spread = jnp.sum(jnp.where(lane == line, per_band, 0.0), axis=0, keepdims=True)
    place = lax.broadcasted_iota(jnp.int32, (8, DIM), 0)
    rab_out[...] = jnp.where(place == head, spread * (0.5 / 64.0 / 4096.0), 0.0)

    for which in (0, 1):
        for rel in (1, 2, 3):
            delivered(rel, which).wait_recv()
    out_ref[...] = land[...]

    for which in (0, 1):
        for rel in (1, 2, 3):
            exchange(rel, which).wait_send()
            deliver(rel, which).wait_send()
    for half in (far, near):
        to_one(half).wait_send()
        to_two(half).wait_send()
        back_one(half).wait_send()
        back_two(half).wait_send()
        back_three(half).wait_send()

        @pl.when(gives_three)
        def _():
            pass_three(half).wait_send()

        @pl.when(gives_four)
        def _():
            pass_four(half).wait_send()

        @pl.when(zp == 5)
        def _():
            to_three(half).wait_send()

        @pl.when(has_four)
        def _():
            back_four(half).wait_send()


def body(queries, keys, values, gates, lengths, rab_steps, out_grad):
    block = (2, 2, HALF, DIM)
    any_space = pl.BlockSpec(memory_space=pl.ANY)
    smem = pl.BlockSpec(memory_space=pltpu.SMEM)
    vmem = pl.BlockSpec(memory_space=pltpu.VMEM)
    dma = pltpu.SemaphoreType.DMA
    landed, rab_part = pl.pallas_call(
        kernel,
        out_shape=(
            jax.ShapeDtypeStruct((2, 2, ROWS, HEADS * DIM), BF16),
            jax.ShapeDtypeStruct((8, DIM), F32),
        ),
        in_specs=[any_space] * 5 + [smem] * 2,
        out_specs=(vmem, vmem),
        scratch_shapes=[
            pltpu.VMEM((2, 2, ROWS, HEADS * DIM), BF16),
            pltpu.VMEM((2, ROWS, HEADS * DIM), BF16),
            pltpu.VMEM((6,) + block, BF16),
            pltpu.VMEM((6,) + block, F32),
            pltpu.VMEM((4,) + block, BF16),
            pltpu.VMEM((5,) + block, BF16),
            pltpu.VMEM((2,) + block, BF16),
            pltpu.VMEM((2, 2, ROWS, HEADS * DIM), BF16),
            pltpu.SMEM((BANDS + 1,), F32),
            pltpu.VMEM((BANDS, 8, HALF), F32),
            pltpu.VMEM((BANDS, 8, HALF), F32),
            dma((5,)),
            dma((3, 2)),
            dma((3, 2)),
            dma((5, 2)),
            dma((4, 2)),
            dma((4, 2)),
            dma((5, 2)),
            dma((3, 2)),
            dma((3, 2)),
        ],
        compiler_params=pltpu.CompilerParams(
            collective_id=0, has_side_effects=True, vmem_limit_bytes=40 * 2**20
        ),
        name="attend",
    )(queries[0], keys[0], values[0], gates[0], out_grad[0], lengths, rab_steps)
    rab_grad = lax.psum(rab_part[:HEADS, :BANDS], ("dp", "seq"))
    row_at = lax.axis_index("seq") * ROWS + jnp.arange(ROWS, dtype=jnp.int32)[:, None]
    attended = jnp.where(row_at < lengths[0], landed[0, 1].astype(F32), 0.0)
    gated = (attended * gates[0].astype(F32)).astype(BF16)
    gate_grad = (attended * out_grad[0].astype(F32)).astype(BF16)
    return gated[None], landed[0, 0][None], landed[1, 0][None], landed[1, 1][None], gate_grad[None], rab_grad


def solution(mesh):
    rows = P("dp", "seq", None)
    return jax.shard_map(
        body,
        mesh=mesh,
        in_specs=(rows, rows, rows, rows, P("dp"), P(), rows),
        out_specs=(rows, rows, rows, rows, rows, P()),
        check_vma=False,
    )
```

time: 597 us -> 198 us (0.33)
  the two profiles are of different devices: /device:TPU:7 before, /device:TPU:1 now
where the time goes in v1:
time: 198 us
  blocking collectives  122 us (62%)
  Pallas kernels  67.7 us (34%)
  local copies, waits for them, and re-layouts  5.96 us (3%)
    psum x1, blocking collectives, body(): rab_grad = lax.psum(rab_part[:HEADS, :BANDS], ('dp', 'seq'))  122 us
    pallas_call x1, Pallas kernels, body(): pl.pallas_call(kernel, out_shape=(jax.ShapeDtypeStruct((2, 2, ROWS, HEADS...  67.7 us
    unnamed x16, local copies, waits for them, and re-layouts  5.2 us

profile of v1, /device:TPU:1, one launch (start us, length us, event | category | flops | bytes accessed | tf_op | source)
XLA Modules:
  0.0 198.0 jit_solution(5780584182253711972)
XLA Ops:
  1.3 0.0 copy-start.7
  1.3 0.7 copy-done.7
  2.0 0.0 copy-start
  2.0 0.9 copy-done
  2.9 0.0 copy-start.2
  2.9 0.9 copy-done.2
  3.8 0.0 copy-start.4
  3.8 0.9 copy-done.4
  4.7 0.0 copy-start.5
  4.7 0.9 copy-done.5
  5.6 0.0 copy-start.6
  5.6 0.9 copy-done.6
  6.5 0.0 copy-start.1
  6.5 0.0 copy-start.3
  6.5 67.7 %attend.1 = (bf16[2,2,128,512]{3,2,1,0:T(8,128)(2,1)S(1)}, f32[8,128]{1,0:T(8,128)S(1)}) custom-call(bf16[128,512]{1,0:T(8,128)(2,1)S(1)} %bitcast.19, bf16[128,512]{1,0:T(8,128)(2,1)S(1)} %bitcast.20, bf16[128,512]{1,0:T(8,128)(2,1)S(1)} %bitcast.21, bf16[128,512]{1,0:T(8,128)(2,1)S(1)} %bitcast.18, bf16[128,512]{1,0:T(8,128)(2,1)S(1)} %bitcast.17, ...), custom_call_target="tpu_custom_call" | custom-call | tf_op jit(solution)/shard_map/attend/pallas_call | solution.py:420
  74.2 122.2 %psum.7 = f32[4,16]{1,0:T(4,128)} all-reduce(f32[4,16]{1,0:T(4,128)S(1)} %slice.19), channel_id=1, replica_groups=mesh['dp'=32,'seq'=32] {'dp','seq'}, use_global_device_ids=true, to_apply=%region_0.0 | all-reduce | flops 64 | bytes 512 | tf_op jit(solution)/shard_map/psum | solution.py:455
  196.4 0.0 copy-done.1
  196.4 0.0 copy-done.3
  196.4 0.8 fusion.3
  197.3 0.8 slice_bitcast_fusion
  (2 shorter events, 0.0 us)
Async XLA Ops:
  1.3 0.7 copy-start.7
  2.0 0.9 copy-start
  2.9 0.9 copy-start.2
  3.8 0.9 copy-start.4
  4.7 0.9 copy-start.5
  5.6 0.9 copy-start.6
  6.5 189.9 %copy-start.1 = (bf16[1,128,512]{2,1,0:T(8,128)(2,1)S(1)}, bf16[1,128,512]{2,1,0:T(8,128)(2,1)}, u32[]{:S(2)}) copy-start(bf16[1,128,512]{2,1,0:T(8,128)(2,1)} %param.13) | copy-start | bytes 393220
  6.5 189.9 %copy-start.3 = (bf16[1,128,512]{2,1,0:T(8,128)(2,1)S(1)}, bf16[1,128,512]{2,1,0:T(8,128)(2,1)}, u32[]{:S(2)}) copy-start(bf16[1,128,512]{2,1,0:T(8,128)(2,1)} %param.10) | copy-start | bytes 393220

commit v2 on v1

--- a/solution.py
+++ b/solution.py
@@ -30,9 +30,11 @@
     q_hbm, k_hbm, v_hbm, gate_hbm, og_hbm, len_ref, rab_ref,
     out_ref, rab_out,
     src, raw, obj, acc, snd, ret, stg, land, csm, low, tot,
-    l_sem, a_s, a_r, f_s, f_r, b_s, b_r, o_s, o_r,
+    msg, got,
+    l_sem, a_s, a_r, f_s, f_r, b_s, b_r, o_s, o_r, r_s, r_r,
 ):
-    sq = lax.axis_index("seq")
+    dp, sq = lax.axis_index("dp"), lax.axis_index("seq")
+    y, xl = dp // 4, dp % 4
     z, xh, c = sq // 4, (sq // 2) % 2, sq % 2
     head = 2 * xh + c
     sign = 1 - 2 * c
@@ -55,8 +57,11 @@
     barrier = pltpu.get_barrier_semaphore()
     for rel in (1, 2, 3):
         pl.semaphore_signal(barrier, inc=1, device_id=at_plane(rel), device_id_type=MESH)
-    for step in (1, -1, 2, -2, 3, -3):
+    for step in range(1, 8):
         pl.semaphore_signal(barrier, inc=1, device_id=at_z(step), device_id_type=MESH)
+        pl.semaphore_signal(barrier, inc=1, device_id={"dp": ((y + step) % 8) * 4 + xl}, device_id_type=MESH)
+    for step in range(1, 4):
+        pl.semaphore_signal(barrier, inc=1, device_id={"dp": y * 4 + (xl + step) % 4}, device_id_type=MESH)
 
     loads = [
         pltpu.make_async_copy(gate_hbm, raw.at[0], l_sem.at[0]),
@@ -79,7 +84,7 @@
     src[0, 1] = jnp.where(row_at < len_ref[0], dgrad, 0.0).astype(BF16)
     for load in loads[2:]:
         load.wait()
-    pl.semaphore_wait(barrier, 9)
+    pl.semaphore_wait(barrier, 20)
 
     def head_cols(which):
         return pl.ds(pl.multiple_of(which * DIM, DIM), DIM)
@@ -125,82 +130,77 @@
         for part in (0, 1):
             obj[which, xh, part, own_rows(c), :] = src[which, part, :, head_cols(head)]
 
-    def move(source, hop, dist, half, kind):
-        return pltpu.make_async_remote_copy(
-            src_ref=obj.at[source, half],
-            dst_ref=obj.at[1 + dist, half],
-            send_sem=f_s.at[kind, half],
-            recv_sem=f_r.at[dist - 1, half],
+    def move(source, hop, dist, half, part, kind):
+        return pltpu.make_async_remote_copy(
+            src_ref=obj.at[source, half, part],
+            dst_ref=obj.at[1 + dist, half, part],
+            send_sem=f_s.at[kind, half, part],
+            recv_sem=f_r.at[dist - 1, half, part],
             device_id=at_z(hop),
             device_id_type=MESH,
         )
 
-    def own_slot(dist):
-        return jnp.where(zp + dist < 8, prim, sec)
-
-    def to_one(half):
-        return move(own_slot(1), 1, 1, half, 0)
-
-    def to_two(half):
-        return move(own_slot(2), 2, 2, half, 1)
-
-    def pass_three(half):
-        return move(3, 1, 3, half, 2)
-
-    def pass_four(half):
-        return move(3, 2, 4, half, 3)
-
-    def to_three(half):
-        return move(sec, 3, 3, half, 4)
-
-    gives_three = zp != 7
-    gives_four = (zp >= 2) & (zp <= 5)
-    has_four = zp >= 4
-
-    def pass_on(half):
-        to_two(half).wait_recv()
-
-        @pl.when(gives_three)
-        def _():
-            pass_three(half).start()
-
-        @pl.when(gives_four)
-        def _():
-            pass_four(half).start()
+    late = jnp.where(zp < 7, prim, sec)
+    jump = jnp.where(zp == 6, 2, 3)
+
+    def to_next(half, part):
+        return move(late, 1, 1, half, part, 0)
+
+    def along(dist, half, part):
+        return move(1 + dist, 1, dist + 1, half, part, dist)
+
+    def across(half, part):
+        return move(sec, jump, jump, half, part, 4)
+
+    def hands_on(dist):
+        return (zp >= 1) & (zp <= 4) if dist == 3 else zp != 7
+
+    has_four = (zp >= 2) & (zp <= 5)
+    jumps = (zp == 5) | (zp == 6)
+
+    def start_both(copy_of, half):
+        for part in (0, 1):
+            copy_of(half, part).start()
+
+    def pass_on(dist, half):
+        for part in (0, 1):
+            move(0, 1, dist, half, part, 0).wait_recv()
+
+            @pl.when(hands_on(dist))
+            def _():
+                along(dist, half, part).start()
+
+    def leave(half):
+        @pl.when(zp != 6)
+        def _():
+            start_both(to_next, half)
+
+        @pl.when(zp == 6)
+        def _():
+            start_both(across, half)
 
     arrival(1, mine).wait_recv()
-    to_two(near).start()
-
-    @pl.when(zp != 6)
-    def _():
-        to_one(near).start()
-
-    arrival(2, mine).wait_recv()
-    arrival(3, mine).wait_recv()
-    to_two(far).start()
-
-    @pl.when(zp != 6)
-    def _():
-        to_one(far).start()
-
+    leave(near)
     acc[...] = jnp.zeros_like(acc)
     low[...] = jnp.zeros_like(low)
     tot[...] = jnp.zeros_like(tot)
-    pass_on(near)
+    pass_on(1, near)
+    arrival(2, mine).wait_recv()
+    arrival(3, mine).wait_recv()
+    leave(far)
+    pass_on(2, near)
+    pass_on(3, near)
+    pass_on(1, far)
     for rel in (1, 2, 3):
         arrival(rel, 1 - mine).wait_recv()
-
-    @pl.when(zp == 6)
-    def _():
-        to_one(near).start()
-        to_one(far).start()
-
-    @pl.when(zp == 5)
-    def _():
-        to_three(near).start()
-        to_three(far).start()
-
-    pass_on(far)
+    for half in (near, far):
+        @pl.when(zp == 6)
+        def _():
+            start_both(to_next, half)
+
+        @pl.when(zp == 5)
+        def _():
+            start_both(across, half)
 
     row = lax.broadcasted_iota(jnp.int32, (HALF, HALF), 0)
     col = lax.broadcasted_iota(jnp.int32, (HALF, HALF), 1)
@@ -233,12 +233,21 @@
     lax.fori_loop(0, 3, diagonal, 0)
 
     def chunk(index, unused):
-        dist = index // 2 + 1
-        half = jnp.where(index % 2 == 0, near, far)
-
-        @pl.when(dist != 2)
-        def _():
-            move(0, 1, dist, half, 0).wait_recv()
+        dist = jnp.where(index >= 6, 4, index % 3 + 1)
+        half = jnp.where((index < 3) | (index == 6), near, far)
+
+        @pl.when(index == 1)
+        def _():
+            pass_on(2, far)
+
+        @pl.when(index == 4)
+        def _():
+            pass_on(3, far)
+
+        @pl.when(index >= 6)
+        def _():
+            for part in (0, 1):
+                move(0, 1, 4, half, part, 0).wait_recv()
 
         slot = 1 + dist
         direct = zp >= dist
@@ -254,46 +263,106 @@
 
     lax.fori_loop(0, jnp.where(has_four, 8, 6), chunk, 0)
 
-    def give_back(dist, hop, place, half):
-        return pltpu.make_async_remote_copy(
-            src_ref=snd.at[dist - 1, half],
-            dst_ref=ret.at[place, half],
-            send_sem=b_s.at[dist - 1, half],
-            recv_sem=b_r.at[place, half],
-            device_id=at_z(-hop),
-            device_id_type=MESH,
-        )
-
-    def back_one(half):
-        return give_back(1, 1, 2, half)
-
-    def back_two(half):
-        return give_back(2, 2, 3, half)
-
-    def back_three(half):
-        first = zp == 0
-        return give_back(3, jnp.where(first, 3, 1), jnp.where(first, 4, 0), half)
-
-    def back_four(half):
-        return give_back(4, 2, 1, half)
-
-    def ready(dist, half):
-        snd[dist - 1, half] = acc[1 + dist, half].astype(BF16)
-
-    def returned(place, half):
-        give_back(1, 1, place, half).wait_recv()
-
-    for half in (far, near):
-        @pl.when(has_four)
-        def _():
-            ready(4, half)
-            back_four(half).start()
-
-        ready(3, half)
-        back_three(half).start()
-    for half in (far, near):
-        ready(1, half)
-        back_one(half).start()
+    def give_back(dist, half, part):
+        jumped = (zp == 0) if dist in (2, 3) else False
+        place = jnp.where(jumped, 4, dist - 1)
+        return pltpu.make_async_remote_copy(
+            src_ref=snd.at[dist - 1, half, part],
+            dst_ref=ret.at[place, half, part],
+            send_sem=b_s.at[dist - 1, half, part],
+            recv_sem=b_r.at[place, half, part],
+            device_id=at_z(jnp.where(jumped, -dist, -1)),
+            device_id_type=MESH,
+        )
+
+    def take_back(slot, place, half, part):
+        pltpu.make_async_remote_copy(
+            src_ref=snd.at[0, half, part],
+            dst_ref=ret.at[place, half, part],
+            send_sem=b_s.at[0, half, part],
+            recv_sem=b_r.at[place, half, part],
+            device_id=at_z(-1),
+            device_id_type=MESH,
+        ).wait_recv()
+        acc[slot, half, part] += ret[place, half, part].astype(F32)
+
+    def send_back(dist):
+        for half in (far, near):
+            for part in (0, 1):
+                if dist < 4:
+                    @pl.when(hands_on(dist))
+                    def _():
+                        take_back(1 + dist, dist, half, part)
+
+                snd[dist - 1, half, part] = acc[1 + dist, half, part].astype(BF16)
+                give_back(dist, half, part).start()
+
+    rows_out = [None] * BANDS
+    running = jnp.zeros((1, HALF), F32)
+    for band in range(BANDS - 1, -1, -1):
+        rows_out[band] = running + jnp.sum(low[band], axis=0, keepdims=True)
+        running = running + jnp.sum(tot[band], axis=0, keepdims=True)
+    per_band = jnp.sum(jnp.concatenate(rows_out, axis=0), axis=1, keepdims=True)
+    lane = lax.broadcasted_iota(jnp.int32, (BANDS, DIM), 1)
+    line = lax.broadcasted_iota(jnp.int32, (BANDS, DIM), 0)
+    spread = jnp.sum(jnp.where(lane == line, per_band, 0.0), axis=0, keepdims=True)
+    place = lax.broadcasted_iota(jnp.int32, (8, DIM), 0)
+    share = jnp.where(place == head, spread * (0.5 / 64.0 / 4096.0), 0.0)
+
+    def stage(phase):
+        if phase == 0:
+            return 8, z, lambda other: {"seq": other * 4 + head}
+        if phase == 1:
+            return 8, y, lambda other: {"dp": other * 4 + xl}
+        if phase == 2:
+            return 4, xl, lambda other: {"dp": y * 4 + other}
+        return 4, head, lambda other: {"seq": z * 4 + other}
+
+    def share_with(phase, step):
+        count, here, place_of = stage(phase)
+        other = (here + step) % count
+        return pltpu.make_async_remote_copy(
+            src_ref=msg.at[phase],
+            dst_ref=got.at[phase, here],
+            send_sem=r_s.at[phase, step],
+            recv_sem=r_r.at[phase, here],
+            device_id=place_of(other),
+            device_id_type=MESH,
+        )
+
+    def shared_by(phase, step):
+        count, here, place_of = stage(phase)
+        other = (here + step) % count
+        return pltpu.make_async_remote_copy(
+            src_ref=msg.at[phase],
+            dst_ref=got.at[phase, other],
+            send_sem=r_s.at[phase, step],
+            recv_sem=r_r.at[phase, other],
+            device_id=place_of(other),
+            device_id_type=MESH,
+        )
+
+    def send_share(phase, value):
+        count, here, _ = stage(phase)
+        msg[phase] = value
+        for step in range(1, count):
+            share_with(phase, step).start()
+        got[phase, here] = value
+
+    def sum_shares(phase):
+        count, _, _ = stage(phase)
+        for step in range(1, count):
+            shared_by(phase, step).wait_recv()
+        total = got[phase, 0]
+        for other in range(1, count):
+            total = total + got[phase, other]
+        return total
+
+    send_share(0, share)
+
+    @pl.when(has_four)
+    def _():
+        send_back(4)
 
     def deliver(rel, which):
         other_x, other_c = plane(rel)
@@ -328,87 +397,62 @@
             for part in (0, 1):
                 land[which, part, :, head_cols(head)] = stg[which, half, part, own_rows(c), :]
 
-    late = own_slot(2)
-    both_late = (zp == 5) | (zp == 6)
-
-    @pl.when(jnp.logical_not(both_late))
+    @pl.when(jnp.logical_not(jumps))
     def _():
         finish(1 - late, far, True)
         finish(1 - late, near, False)
 
-    for half in (far, near):
-        @pl.when(gives_three)
-        def _():
-            returned(0, half)
-            acc[3, half] += ret[0, half].astype(F32)
-
-        @pl.when(gives_four)
-        def _():
-            returned(1, half)
-            acc[3, half] += ret[1, half].astype(F32)
-
-        ready(2, half)
-        back_two(half).start()
+    send_back(3)
+    send_share(1, sum_shares(0))
+    send_back(2)
+    send_back(1)
     for half, is_far in ((far, True), (near, False)):
-        returned(2, half)
-        acc[own_slot(1), half] += ret[2, half].astype(F32)
-        returned(3, half)
-        acc[late, half] += ret[3, half].astype(F32)
-
-        @pl.when(zp == 5)
-        def _():
-            returned(4, half)
-            acc[sec, half] += ret[4, half].astype(F32)
+        for part in (0, 1):
+            take_back(late, 0, half, part)
+
+        @pl.when(jumps)
+        def _():
+            for part in (0, 1):
+                take_back(sec, 4, half, part)
 
         finish(late, half, is_far)
 
-        @pl.when(both_late)
+        @pl.when(jumps)
         def _():
             finish(1 - late, half, is_far)
 
-    rows_out = [None] * BANDS
-    running = jnp.zeros((1, HALF), F32)
-    for band in range(BANDS - 1, -1, -1):
-        rows_out[band] = running + jnp.sum(low[band], axis=0, keepdims=True)
-        running = running + jnp.sum(tot[band], axis=0, keepdims=True)
-    per_band = jnp.sum(jnp.concatenate(rows_out, axis=0), axis=1, keepdims=True)
-    lane = lax.broadcasted_iota(jnp.int32, (BANDS, DIM), 1)
-    line = lax.broadcasted_iota(jnp.int32, (BANDS, DIM), 0)
-    spread = jnp.sum(jnp.where(lane == line, per_band, 0.0), axis=0, keepdims=True)
-    place = lax.broadcasted_iota(jnp.int32, (8, DIM), 0)
-    rab_out[...] = jnp.where(place == head, spread * (0.5 / 64.0 / 4096.0), 0.0)
+        send_share(2 if is_far else 3, sum_shares(1 if is_far else 2))
 
     for which in (0, 1):
         for rel in (1, 2, 3):
             delivered(rel, which).wait_recv()
+    rab_out[...] = sum_shares(3)
     out_ref[...] = land[...]
+    for phase in range(4):
+        for step in range(1, stage(phase)[0]):
+            share_with(phase, step).wait_send()
 
     for which in (0, 1):
         for rel in (1, 2, 3):
             exchange(rel, which).wait_send()
             deliver(rel, which).wait_send()
     for half in (far, near):
-        to_one(half).wait_send()
-        to_two(half).wait_send()
-        back_one(half).wait_send()
-        back_two(half).wait_send()
-        back_three(half).wait_send()
-
-        @pl.when(gives_three)
-        def _():
-            pass_three(half).wait_send()
-
-        @pl.when(gives_four)
-        def _():
-            pass_four(half).wait_send()
-
-        @pl.when(zp == 5)
-        def _():
-            to_three(half).wait_send()
-
-        @pl.when(has_four)
-        def _():
-            back_four(half).wait_send()
+        for part in (0, 1):
+            to_next(half, part).wait_send()
+            for dist in (1, 2, 3):
+                give_back(dist, half, part).wait_send()
+
+                @pl.when(hands_on(dist))
+                def _():
+                    along(dist, half, part).wait_send()
+
+            @pl.when(jumps)
+            def _():
+                across(half, part).wait_send()
+
+            @pl.when(has_four)
+            def _():
+                give_back(4, half, part).wait_send()
 
 
 def body(queries, keys, values, gates, lengths, rab_steps, out_grad):
@@ -437,22 +481,26 @@
             pltpu.SMEM((BANDS + 1,), F32),
             pltpu.VMEM((BANDS, 8, HALF), F32),
             pltpu.VMEM((BANDS, 8, HALF), F32),
+            pltpu.VMEM((4, 8, DIM), F32),
+            pltpu.VMEM((4, 8, 8, DIM), F32),
             dma((5,)),
             dma((3, 2)),
             dma((3, 2)),
-            dma((5, 2)),
-            dma((4, 2)),
-            dma((4, 2)),
-            dma((5, 2)),
+            dma((5, 2, 2)),
+            dma((4, 2, 2)),
+            dma((4, 2, 2)),
+            dma((5, 2, 2)),
             dma((3, 2)),
             dma((3, 2)),
+            dma((4, 8)),
+            dma((4, 8)),
         ],
         compiler_params=pltpu.CompilerParams(
-            collective_id=0, has_side_effects=True, vmem_limit_bytes=40 * 2**20
+            collective_id=0, has_side_effects=True, vmem_limit_bytes=60 * 2**20
         ),
         name="attend",
     )(queries[0], keys[0], values[0], gates[0], out_grad[0], lengths, rab_steps)
-    rab_grad = lax.psum(rab_part[:HEADS, :BANDS], ("dp", "seq"))
+    rab_grad = rab_part[:HEADS, :BANDS]
     row_at = lax.axis_index("seq") * ROWS + jnp.arange(ROWS, dtype=jnp.int32)[:, None]
     attended = jnp.where(row_at < lengths[0], landed[0, 1].astype(F32), 0.0)
     gated = (attended * gates[0].astype(F32)).astype(BF16)

time: 198 us -> 95.6 us (0.48)
  blocking collectives: 122 us -> 0 us
  Pallas kernels: 67.7 us -> 90.3 us
  local copies, waits for them, and re-layouts: 5.96 us -> 2.07 us
    psum x1 -> x0, blocking collectives: 122 us -> none  [body(): rab_grad = lax.psum(rab_part[:HEADS, :BANDS], ('dp', 'seq'))]
    pallas_call x1, Pallas kernels: 67.7 us -> 90.3 us  [body(): pl.pallas_call(kernel, out_shape=(jax.ShapeDtypeStruct((2, 2, ROWS, HEADS...]
    unnamed x16 -> x6, local copies, waits for them, and re-layouts: 5.2 us -> 0.02 us
where the time goes in v2:
time: 95.6 us; the launch traced here: 95.4 us
  Pallas kernels  90.3 us (94%)
  local copies, waits for them, and re-layouts  2.07 us (2%)
  other arithmetic  1.74 us (2%)
  between operations  1.32 us (1%)
    pallas_call x1, Pallas kernels, body(): pl.pallas_call(kernel, out_shape=(jax.ShapeDtypeStruct((2, 2, ROWS, HEADS...  90.3 us

profile of v2, /device:TPU:1, one launch (start us, length us, event | category | flops | bytes accessed | tf_op | source)
XLA Modules:
  0.0 95.4 jit_solution(12024627118339654587)
XLA Ops:
  1.3 0.0 copy-start.1
  1.3 0.0 copy-start.2
  1.3 90.3 %attend.1 = (bf16[2,2,128,512]{3,2,1,0:T(8,128)(2,1)}, f32[8,128]{1,0:T(8,128)}) custom-call(bf16[128,512]{1,0:T(8,128)(2,1)} %bitcast.19, bf16[128,512]{1,0:T(8,128)(2,1)} %bitcast.20, bf16[128,512]{1,0:T(8,128)(2,1)} %bitcast.21, bf16[128,512]{1,0:T(8,128)(2,1)} %bitcast.18, bf16[128,512]{1,0:T(8,128)(2,1)} %bitcast.17, s32[1]{0:T(128)} %copy.13.len_ref, ...), custom_call_target="tpu_custom_call" | custom-call | tf_op jit(solution)/shard_map/attend/pallas_call | solution.py:464
  91.6 0.0 copy-start
  91.6 1.3 %slice.19 = f32[4,16]{1,0:T(4,128)} slice(f32[8,128]{1,0:T(8,128)} %get-tuple-element.9), slice={[0:4], [0:16]} | slice | bytes 512 | tf_op jit(solution)/shard_map/slice | solution.py:503
  92.9 0.0 copy-done.1
  92.9 0.0 copy-done.2
  92.9 1.7 %fusion.3 = (bf16[1,128,512]{2,1,0:T(8,128)(2,1)}, bf16[1,128,512]{2,1,0:T(8,128)(2,1)}) fusion(bf16[1,128,512]{2,1,0:T(8,128)(2,1)S(1)} %copy-done.1, pred[128]{0:T(512)(128)(4,1)S(1)} %add_compare_fusion, bf16[2,2,128,512]{3,2,1,0:T(8,128)(2,1)} %get-tuple-element.8, bf16[1,128,512]{2,1,0:T(8,128)(2,1)S(1)} %copy-done.2), kind=kLoop, calls=%fused_computation.4 | loop fusion | flops 524288 | bytes 655488 | tf_op jit(solution)/shard_map/convert_element_type | solution.py:507
  94.6 0.0 copy-done
  94.7 0.8 slice_bitcast_fusion
  (1 shorter events, 0.0 us)
Async XLA Ops:
  1.3 91.6 %copy-start.1 = (bf16[1,128,512]{2,1,0:T(8,128)(2,1)S(1)}, bf16[1,128,512]{2,1,0:T(8,128)(2,1)}, u32[]{:S(2)}) copy-start(bf16[1,128,512]{2,1,0:T(8,128)(2,1)} %param.13) | copy-start | bytes 393220
  1.3 91.6 %copy-start.2 = (bf16[1,128,512]{2,1,0:T(8,128)(2,1)S(1)}, bf16[1,128,512]{2,1,0:T(8,128)(2,1)}, u32[]{:S(2)}) copy-start(bf16[1,128,512]{2,1,0:T(8,128)(2,1)} %param.10) | copy-start | bytes 393220
  91.6 3.1 %copy-start = (bf16[2,2,128,512]{3,2,1,0:T(8,128)(2,1)S(1)}, bf16[2,2,128,512]{3,2,1,0:T(8,128)(2,1)}, u32[]{:S(2)}) copy-start(bf16[2,2,128,512]{3,2,1,0:T(8,128)(2,1)} %get-tuple-element.8) | copy-start | bytes 1572868

commit v3 on v2

--- a/solution.py
+++ b/solution.py
@@ -130,77 +130,82 @@
         for part in (0, 1):
             obj[which, xh, part, own_rows(c), :] = src[which, part, :, head_cols(head)]
 
-    def move(source, hop, dist, half, part, kind):
-        return pltpu.make_async_remote_copy(
-            src_ref=obj.at[source, half, part],
-            dst_ref=obj.at[1 + dist, half, part],
-            send_sem=f_s.at[kind, half, part],
-            recv_sem=f_r.at[dist - 1, half, part],
+    def move(source, hop, dist, half, kind):
+        return pltpu.make_async_remote_copy(
+            src_ref=obj.at[source, half],
+            dst_ref=obj.at[1 + dist, half],
+            send_sem=f_s.at[kind, half],
+            recv_sem=f_r.at[dist - 1, half],
             device_id=at_z(hop),
             device_id_type=MESH,
         )
 
     late = jnp.where(zp < 7, prim, sec)
-    jump = jnp.where(zp == 6, 2, 3)
-
-    def to_next(half, part):
-        return move(late, 1, 1, half, part, 0)
-
-    def along(dist, half, part):
-        return move(1 + dist, 1, dist + 1, half, part, dist)
-
-    def across(half, part):
-        return move(sec, jump, jump, half, part, 4)
-
-    def hands_on(dist):
-        return (zp >= 1) & (zp <= 4) if dist == 3 else zp != 7
-
+
+    def to_one(half):
+        return move(late, 1, 1, half, 0)
+
+    def to_two(half):
+        return move(jnp.where(zp < 6, prim, sec), 2, 2, half, 1)
+
+    def pass_three(half):
+        return move(3, 1, 3, half, 2)
+
+    def pass_four(half):
+        return move(3, 2, 4, half, 3)
+
+    def to_three(half):
+        return move(sec, 3, 3, half, 4)
+
+    gives_three = zp != 7
+    gives_four = zp <= 3
     has_four = (zp >= 2) & (zp <= 5)
     jumps = (zp == 5) | (zp == 6)
 
-    def start_both(copy_of, half):
-        for part in (0, 1):
-            copy_of(half, part).start()
-
-    def pass_on(dist, half):
-        for part in (0, 1):
-            move(0, 1, dist, half, part, 0).wait_recv()
-
-            @pl.when(hands_on(dist))
-            def _():
-                along(dist, half, part).start()
+    def sums_up(dist):
+        return (zp >= 1) & (zp <= 4) if dist == 3 else zp != 7
+
+    def pass_on(half):
+        move(0, 2, 2, half, 1).wait_recv()
+
+        @pl.when(gives_three)
+        def _():
+            pass_three(half).start()
+
+        @pl.when(gives_four)
+        def _():
+            pass_four(half).start()
 
     def leave(half):
+        to_two(half).start()
+
         @pl.when(zp != 6)
         def _():
-            start_both(to_next, half)
-
-        @pl.when(zp == 6)
-        def _():
-            start_both(across, half)
+            to_one(half).start()
 
     arrival(1, mine).wait_recv()
     leave(near)
     acc[...] = jnp.zeros_like(acc)
     low[...] = jnp.zeros_like(low)
     tot[...] = jnp.zeros_like(tot)
-    pass_on(1, near)
     arrival(2, mine).wait_recv()
     arrival(3, mine).wait_recv()
     leave(far)
-    pass_on(2, near)
-    pass_on(3, near)
-    pass_on(1, far)
+    pass_on(near)
     for rel in (1, 2, 3):
         arrival(rel, 1 - mine).wait_recv()
-    for half in (near, far):
-        @pl.when(zp == 6)
-        def _():
-            start_both(to_next, half)
-
-        @pl.when(zp == 5)
-        def _():
-            start_both(across, half)
+
+    @pl.when(zp == 6)
+    def _():
+        to_one(near).start()
+        to_one(far).start()
+
+    @pl.when(zp == 5)
+    def _():
+        to_three(near).start()
+        to_three(far).start()
+
+    pass_on(far)
 
     row = lax.broadcasted_iota(jnp.int32, (HALF, HALF), 0)
     col = lax.broadcasted_iota(jnp.int32, (HALF, HALF), 1)
@@ -233,21 +238,12 @@
     lax.fori_loop(0, 3, diagonal, 0)
 
     def chunk(index, unused):
-        dist = jnp.where(index >= 6, 4, index % 3 + 1)
-        half = jnp.where((index < 3) | (index == 6), near, far)
-
-        @pl.when(index == 1)
-        def _():
-            pass_on(2, far)
-
-        @pl.when(index == 4)
-        def _():
-            pass_on(3, far)
-
-        @pl.when(index >= 6)
-        def _():
-            for part in (0, 1):
-                move(0, 1, 4, half, part, 0).wait_recv()
+        dist = index // 2 + 1
+        half = jnp.where(index % 2 == 0, near, far)
+
+        @pl.when(dist != 2)
+        def _():
+            move(0, 1, dist, half, 0).wait_recv()
 
         slot = 1 + dist
         direct = zp >= dist
@@ -290,7 +286,7 @@
         for half in (far, near):
             for part in (0, 1):
                 if dist < 4:
-                    @pl.when(hands_on(dist))
+                    @pl.when(sums_up(dist))
                     def _():
                         take_back(1 + dist, dist, half, part)
 
@@ -313,10 +309,10 @@
         if phase == 0:
             return 8, z, lambda other: {"seq": other * 4 + head}
         if phase == 1:
-            return 8, y, lambda other: {"dp": other * 4 + xl}
+            return 4, head, lambda other: {"seq": z * 4 + other}
         if phase == 2:
             return 4, xl, lambda other: {"dp": y * 4 + other}
-        return 4, head, lambda other: {"seq": z * 4 + other}
+        return 8, y, lambda other: {"dp": other * 4 + xl}
 
     def share_with(phase, step):
         count, here, place_of = stage(phase)
@@ -406,6 +402,7 @@
     send_share(1, sum_shares(0))
     send_back(2)
     send_back(1)
+    send_share(2, sum_shares(1))
     for half, is_far in ((far, True), (near, False)):
         for part in (0, 1):
             take_back(late, 0, half, part)
@@ -421,8 +418,7 @@
         def _():
             finish(1 - late, half, is_far)
 
-        send_share(2 if is_far else 3, sum_shares(1 if is_far else 2))
-
+    send_share(3, sum_shares(2))
     for which in (0, 1):
         for rel in (1, 2, 3):
             delivered(rel, which).wait_recv()
@@ -437,18 +433,24 @@
             exchange(rel, which).wait_send()
             deliver(rel, which).wait_send()
     for half in (far, near):
+        to_one(half).wait_send()
+        to_two(half).wait_send()
+
+        @pl.when(gives_three)
+        def _():
+            pass_three(half).wait_send()
+
+        @pl.when(gives_four)
+        def _():
+            pass_four(half).wait_send()
+
+        @pl.when(zp == 5)
+        def _():
+            to_three(half).wait_send()
+
         for part in (0, 1):
-            to_next(half, part).wait_send()
             for dist in (1, 2, 3):
                 give_back(dist, half, part).wait_send()
-
-                @pl.when(hands_on(dist))
-                def _():
-                    along(dist, half, part).wait_send()
-
-            @pl.when(jumps)
-            def _():
-                across(half, part).wait_send()
 
             @pl.when(has_four)
             def _():
@@ -486,8 +488,8 @@
             dma((5,)),
             dma((3, 2)),
             dma((3, 2)),
-            dma((5, 2, 2)),
-            dma((4, 2, 2)),
+            dma((5, 2)),
+            dma((4, 2)),
             dma((4, 2, 2)),
             dma((5, 2, 2)),
             dma((3, 2)),

time: 95.6 us -> 81.4 us (0.85)
  the two profiles are of different devices: /device:TPU:1 before, /device:TPU:14 now
where the time goes in v3:
time: 81.4 us; the launch traced here: 81.1 us
  Pallas kernels  76 us (93%)
  local copies, waits for them, and re-layouts  2.07 us (3%)
  other arithmetic  1.74 us (2%)
  between operations  1.32 us (2%)
    pallas_call x1, Pallas kernels, body(): pl.pallas_call(kernel, out_shape=(jax.ShapeDtypeStruct((2, 2, ROWS, HEADS...  76 us
    convert_element_type x1, other arithmetic, body(): gate_grad = (attended * out_grad[0].astype(F32)).astype(BF16)  1.74 us

profile of v3, /device:TPU:14, one launch (start us, length us, event | category | flops | bytes accessed | tf_op | source)
XLA Modules:
  0.0 81.1 jit_solution(13480381493176995588)
XLA Ops:
  1.3 0.0 copy-start.1
  1.3 0.0 copy-start.2
  1.3 76.0 %attend.1 = (bf16[2,2,128,512]{3,2,1,0:T(8,128)(2,1)}, f32[8,128]{1,0:T(8,128)}) custom-call(bf16[128,512]{1,0:T(8,128)(2,1)} %bitcast.19, bf16[128,512]{1,0:T(8,128)(2,1)} %bitcast.20, bf16[128,512]{1,0:T(8,128)(2,1)} %bitcast.21, bf16[128,512]{1,0:T(8,128)(2,1)} %bitcast.18, bf16[128,512]{1,0:T(8,128)(2,1)} %bitcast.17, s32[1]{0:T(128)} %copy.13.len_ref, ...), custom_call_target="tpu_custom_call" | custom-call | tf_op jit(solution)/shard_map/attend/pallas_call | solution.py:466
  77.3 0.0 copy-start
  77.3 1.3 %slice.19 = f32[4,16]{1,0:T(4,128)} slice(f32[8,128]{1,0:T(8,128)} %get-tuple-element.9), slice={[0:4], [0:16]} | slice | bytes 512 | tf_op jit(solution)/shard_map/slice | solution.py:505
  78.7 0.0 copy-done.1
  78.7 0.0 copy-done.2
  78.7 1.7 %fusion.3 = (bf16[1,128,512]{2,1,0:T(8,128)(2,1)}, bf16[1,128,512]{2,1,0:T(8,128)(2,1)}) fusion(bf16[1,128,512]{2,1,0:T(8,128)(2,1)S(1)} %copy-done.1, pred[128]{0:T(512)(128)(4,1)S(1)} %add_compare_fusion, bf16[2,2,128,512]{3,2,1,0:T(8,128)(2,1)} %get-tuple-element.8, bf16[1,128,512]{2,1,0:T(8,128)(2,1)S(1)} %copy-done.2), kind=kLoop, calls=%fused_computation.4 | loop fusion | flops 524288 | bytes 655488 | tf_op jit(solution)/shard_map/convert_element_type | solution.py:509
  80.4 0.0 copy-done
  80.4 0.8 slice_bitcast_fusion
  (1 shorter events, 0.0 us)
Async XLA Ops:
  1.3 77.4 %copy-start.1 = (bf16[1,128,512]{2,1,0:T(8,128)(2,1)S(1)}, bf16[1,128,512]{2,1,0:T(8,128)(2,1)}, u32[]{:S(2)}) copy-start(bf16[1,128,512]{2,1,0:T(8,128)(2,1)} %param.13) | copy-start | bytes 393220
  1.3 77.4 %copy-start.2 = (bf16[1,128,512]{2,1,0:T(8,128)(2,1)S(1)}, bf16[1,128,512]{2,1,0:T(8,128)(2,1)}, u32[]{:S(2)}) copy-start(bf16[1,128,512]{2,1,0:T(8,128)(2,1)} %param.10) | copy-start | bytes 393220
  77.3 3.1 %copy-start = (bf16[2,2,128,512]{3,2,1,0:T(8,128)(2,1)S(1)}, bf16[2,2,128,512]{3,2,1,0:T(8,128)(2,1)}, u32[]{:S(2)}) copy-start(bf16[2,2,128,512]{3,2,1,0:T(8,128)(2,1)} %get-tuple-element.8) | copy-start | bytes 1572868

commit v4 on v3

--- a/solution.py
+++ b/solution.py
@@ -259,39 +259,38 @@
 
     lax.fori_loop(0, jnp.where(has_four, 8, 6), chunk, 0)
 
-    def give_back(dist, half, part):
-        jumped = (zp == 0) if dist in (2, 3) else False
+    def give_back(dist, half):
+        jumped = (zp == 0) if dist == 3 else False
+        hop = 2 if dist == 2 else jnp.where(jumped, 3, 1)
         place = jnp.where(jumped, 4, dist - 1)
         return pltpu.make_async_remote_copy(
-            src_ref=snd.at[dist - 1, half, part],
-            dst_ref=ret.at[place, half, part],
-            send_sem=b_s.at[dist - 1, half, part],
-            recv_sem=b_r.at[place, half, part],
-            device_id=at_z(jnp.where(jumped, -dist, -1)),
-            device_id_type=MESH,
-        )
-
-    def take_back(slot, place, half, part):
+            src_ref=snd.at[dist - 1, half],
+            dst_ref=ret.at[place, half],
+            send_sem=b_s.at[dist - 1, half],
+            recv_sem=b_r.at[place, half],
+            device_id=at_z(-hop),
+            device_id_type=MESH,
+        )
+
+    def take_back(slot, place, half):
         pltpu.make_async_remote_copy(
-            src_ref=snd.at[0, half, part],
-            dst_ref=ret.at[place, half, part],
-            send_sem=b_s.at[0, half, part],
-            recv_sem=b_r.at[place, half, part],
+            src_ref=snd.at[0, half],
+            dst_ref=ret.at[place, half],
+            send_sem=b_s.at[0, half],
+            recv_sem=b_r.at[place, half],
             device_id=at_z(-1),
             device_id_type=MESH,
         ).wait_recv()
-        acc[slot, half, part] += ret[place, half, part].astype(F32)
-
-    def send_back(dist):
-        for half in (far, near):
-            for part in (0, 1):
-                if dist < 4:
-                    @pl.when(sums_up(dist))
-                    def _():
-                        take_back(1 + dist, dist, half, part)
-
-                snd[dist - 1, half, part] = acc[1 + dist, half, part].astype(BF16)
-                give_back(dist, half, part).start()
+        acc[slot, half] += ret[place, half].astype(F32)
+
+    def send_back(dist, half):
+        if dist in (2, 3):
+            @pl.when(sums_up(dist))
+            def _():
+                take_back(1 + dist, dist, half)
+
+        snd[dist - 1, half] = acc[1 + dist, half].astype(BF16)
+        give_back(dist, half).start()
 
     rows_out = [None] * BANDS
     running = jnp.zeros((1, HALF), F32)
@@ -356,9 +355,12 @@
 
     send_share(0, share)
 
-    @pl.when(has_four)
-    def _():
-        send_back(4)
+    for half in (far, near):
+        @pl.when(has_four)
+        def _():
+            send_back(4, half)
+
+        send_back(1, half)
 
     def deliver(rel, which):
         other_x, other_c = plane(rel)
@@ -398,19 +400,19 @@
         finish(1 - late, far, True)
         finish(1 - late, near, False)
 
-    send_back(3)
+    send_back(3, far)
+    send_back(3, near)
     send_share(1, sum_shares(0))
-    send_back(2)
-    send_back(1)
+    send_back(2, far)
+    send_back(2, near)
     send_share(2, sum_shares(1))
     for half, is_far in ((far, True), (near, False)):
-        for part in (0, 1):
-            take_back(late, 0, half, part)
-
-        @pl.when(jumps)
-        def _():
-            for part in (0, 1):
-                take_back(sec, 4, half, part)
+        take_back(late, 0, half)
+        take_back(jnp.where(zp < 6, prim, sec), 1, half)
+
+        @pl.when(zp == 5)
+        def _():
+            take_back(sec, 4, half)
 
         finish(late, half, is_far)
 
@@ -448,13 +450,23 @@
         def _():
             to_three(half).wait_send()
 
-        for part in (0, 1):
-            for dist in (1, 2, 3):
-                give_back(dist, half, part).wait_send()
-
-            @pl.when(has_four)
-            def _():
-                give_back(4, half, part).wait_send()
+        for dist in (1, 2, 3):
+            give_back(dist, half).wait_send()
+
+        @pl.when(has_four)
+        def _():
+            give_back(4, half).wait_send()
+
+
+def closing(landed, rab_in, gate, outgrad, len_ref, gated, q_grad, k_grad, v_grad, gate_grad, rab_grad):
+    row_at = lax.axis_index("seq") * ROWS + lax.broadcasted_iota(jnp.int32, (ROWS, HEADS * DIM), 0)
+    attended = jnp.where(row_at < len_ref[0], landed[0, 1].astype(F32), 0.0)
+    gated[...] = (attended * gate[...].astype(F32)).astype(BF16)
+    gate_grad[...] = (attended * outgrad[...].astype(F32)).astype(BF16)
+    q_grad[...] = landed[0, 0]
+    k_grad[...] = landed[1, 0]
+    v_grad[...] = landed[1, 1]
+    rab_grad[...] = rab_in[:HEADS, :BANDS]
 
 
 def body(queries, keys, values, gates, lengths, rab_steps, out_grad):
@@ -490,8 +502,8 @@
             dma((3, 2)),
             dma((5, 2)),
             dma((4, 2)),
-            dma((4, 2, 2)),
-            dma((5, 2, 2)),
+            dma((4, 2)),
+            dma((5, 2)),
             dma((3, 2)),
             dma((3, 2)),
             dma((4, 8)),
@@ -502,12 +514,15 @@
         ),
         name="attend",
     )(queries[0], keys[0], values[0], gates[0], out_grad[0], lengths, rab_steps)
-    rab_grad = rab_part[:HEADS, :BANDS]
-    row_at = lax.axis_index("seq") * ROWS + jnp.arange(ROWS, dtype=jnp.int32)[:, None]
-    attended = jnp.where(row_at < lengths[0], landed[0, 1].astype(F32), 0.0)
-    gated = (attended * gates[0].astype(F32)).astype(BF16)
-    gate_grad = (attended * out_grad[0].astype(F32)).astype(BF16)
-    return gated[None], landed[0, 0][None], landed[1, 0][None], landed[1, 1][None], gate_grad[None], rab_grad
+    shape = jax.ShapeDtypeStruct((ROWS, HEADS * DIM), BF16)
+    outs = pl.pallas_call(
+        closing,
+        out_shape=(shape,) * 5 + (jax.ShapeDtypeStruct((HEADS, BANDS), F32),),
+        in_specs=[vmem] * 4 + [smem],
+        out_specs=(vmem,) * 6,
+        name="closing",
+    )(landed, rab_part, gates[0], out_grad[0], lengths)
+    return tuple(out[None] for out in outs[:5]) + (outs[5],)
 
 
 def solution(mesh):

time: 81.4 us -> 79.1 us (0.972)
  the two profiles are of different devices: /device:TPU:14 before, /device:TPU:1 now
where the time goes in v4:
time: 79.1 us; the launch traced here: 78.1 us
  Pallas kernels  76.8 us (97%)
  between operations  1.29 us (2%)
    pallas_call x1, Pallas kernels, body(): pl.pallas_call(kernel, out_shape=(jax.ShapeDtypeStruct((2, 2, ROWS, HEADS...  74.9 us
    pallas_call x1, Pallas kernels, body(): pl.pallas_call(closing, out_shape=(shape,) * 5 + (jax.ShapeDtypeStruct((H...  1.95 us

profile of v4, /device:TPU:1, one launch (start us, length us, event | category | flops | bytes accessed | tf_op | source)
XLA Modules:
  0.0 78.1 jit_solution(718366784854894287)
XLA Ops:
  1.3 74.9 %attend.1 = (bf16[2,2,128,512]{3,2,1,0:T(8,128)(2,1)}, f32[8,128]{1,0:T(8,128)}) custom-call(bf16[128,512]{1,0:T(8,128)(2,1)} %bitcast.14, bf16[128,512]{1,0:T(8,128)(2,1)} %bitcast.15, bf16[128,512]{1,0:T(8,128)(2,1)} %bitcast.16, bf16[128,512]{1,0:T(8,128)(2,1)} %bitcast.10, bf16[128,512]{1,0:T(8,128)(2,1)} %bitcast.12, s32[1]{0:T(128)S(6)} %copy.13.len_ref, ...), custom_call_target="tpu_custom_call" | custom-call | tf_op jit(solution)/shard_map/attend/pallas_call | solution.py:478
  76.2 2.0 %closing.1 = (bf16[128,512]{1,0:T(8,128)(2,1)}, bf16[128,512]{1,0:T(8,128)(2,1)}, bf16[128,512]{1,0:T(8,128)(2,1)}, bf16[128,512]{1,0:T(8,128)(2,1)}, bf16[128,512]{1,0:T(8,128)(2,1)}, /*index=5*/f32[4,16]{1,0:T(4,128)}) custom-call(bf16[2,2,128,512]{3,2,1,0:T(8,128)(2,1)} %get-tuple-element.14.landed, f32[8,128]{1,0:T(8,128)} %get-tuple-element.15.rab_in, ...), custom_call_target="tpu_custom_call" | custom-call | tf_op jit(solution)/shard_map/closing/pallas_call | solution.py:518

commit v5 on v4

--- a/solution.py
+++ b/solution.py
@@ -192,6 +192,7 @@
     arrival(3, mine).wait_recv()
     leave(far)
     pass_on(near)
+    pass_on(far)
     for rel in (1, 2, 3):
         arrival(rel, 1 - mine).wait_recv()
 
@@ -204,8 +205,6 @@
     def _():
         to_three(near).start()
         to_three(far).start()
-
-    pass_on(far)
 
     row = lax.broadcasted_iota(jnp.int32, (HALF, HALF), 0)
     col = lax.broadcasted_iota(jnp.int32, (HALF, HALF), 1)

time: 79.1 us -> 79.4 us (level)
  Pallas kernels: 76.8 us -> 77.9 us
    pallas_call x1, Pallas kernels: 74.9 us -> 75.9 us  [body(): pl.pallas_call(kernel, out_shape=(jax.ShapeDtypeStruct((2, 2, ROWS, HEADS...]
where the time goes in v5:
time: 79.4 us; the launch traced here: 79.1 us
  Pallas kernels  77.9 us (98%)
  between operations  1.29 us (2%)
    pallas_call x1, Pallas kernels, body(): pl.pallas_call(kernel, out_shape=(jax.ShapeDtypeStruct((2, 2, ROWS, HEADS...  75.9 us
    pallas_call x1, Pallas kernels, body(): pl.pallas_call(closing, out_shape=(shape,) * 5 + (jax.ShapeDtypeStruct((H...  1.95 us

profile of v5, /device:TPU:1, one launch (start us, length us, event | category | flops | bytes accessed | tf_op | source)
XLA Modules:
  0.0 79.1 jit_solution(10131173485914961937)
XLA Ops:
  1.3 75.9 %attend.1 = (bf16[2,2,128,512]{3,2,1,0:T(8,128)(2,1)}, f32[8,128]{1,0:T(8,128)}) custom-call(bf16[128,512]{1,0:T(8,128)(2,1)} %bitcast.14, bf16[128,512]{1,0:T(8,128)(2,1)} %bitcast.15, bf16[128,512]{1,0:T(8,128)(2,1)} %bitcast.16, bf16[128,512]{1,0:T(8,128)(2,1)} %bitcast.10, bf16[128,512]{1,0:T(8,128)(2,1)} %bitcast.12, s32[1]{0:T(128)S(6)} %copy.13.len_ref, ...), custom_call_target="tpu_custom_call" | custom-call | tf_op jit(solution)/shard_map/attend/pallas_call | solution.py:477
  77.2 2.0 %closing.1 = (bf16[128,512]{1,0:T(8,128)(2,1)}, bf16[128,512]{1,0:T(8,128)(2,1)}, bf16[128,512]{1,0:T(8,128)(2,1)}, bf16[128,512]{1,0:T(8,128)(2,1)}, bf16[128,512]{1,0:T(8,128)(2,1)}, /*index=5*/f32[4,16]{1,0:T(4,128)}) custom-call(bf16[2,2,128,512]{3,2,1,0:T(8,128)(2,1)} %get-tuple-element.14.landed, f32[8,128]{1,0:T(8,128)} %get-tuple-element.15.rab_in, ...), custom_call_target="tpu_custom_call" | custom-call | tf_op jit(solution)/shard_map/closing/pallas_call | solution.py:517
